TPU v7x, 32 devices: a whole 2x2x4 slice. The times are simulated.
32 devices in a mesh: grp: 4 (over y, x), seq: 4 (over z), mlp: 2 (over core).
Axes of the slice: x: 2, y: 2, z: 4, core: 2. Of those that a mesh axis runs over, the one named last changes fastest.
Arguments:
- queries: bfloat16 [16, 4, 4096], P('grp'), may hold values from -6 to 6
- new_keys: bfloat16 [16, 4, 4096], P(('grp', 'seq')), may hold values from -6 to 6
- new_values: bfloat16 [16, 4, 4096], P(('grp', 'seq')), may hold values from -6 to 6
- prefix_keys: bfloat16 [4, 2048, 4096], P('grp', ('seq', 'mlp')), may hold values from -250 to 250
- prefix_values: bfloat16 [4, 2048, 4096], P('grp', ('seq', 'mlp')), may hold values from -6 to 6
- tail_keys: bfloat16 [16, 256, 4096], P(('grp', 'seq'), 'mlp'), may hold values from -6 to 6
- tail_values: bfloat16 [16, 256, 4096], P(('grp', 'seq'), 'mlp'), may hold values from -6 to 6
- prefix_len: int32 [4], P('grp'), may hold values from 1 to 2048, as said below
- tail_len: int32 [16], P('grp'), may hold values from 0 to 256, as said below
- resid: bfloat16 [16, 4, 4096], P('grp', None, ('seq', 'mlp')), may hold values from -12 to 12
- w_out: bfloat16 [4096, 4096], P(None, ('seq', 'mlp')), may hold values from -0.09375 to 0.09375
- ln_gain: bfloat16 [4096], P(('seq', 'mlp')), may hold values from 0.25 to 1.75
- w_up: bfloat16 [4096, 16384], P(('seq', 'mlp'), 'grp'), may hold values from -0.09375 to 0.09375
- w_down: bfloat16 [16384, 4096], P('grp', ('seq', 'mlp')), may hold values from -0.046875 to 0.046875
Outputs:
- out: float32 [16, 4, 4096], P('grp', None, ('seq', 'mlp'))
Inputs may be any that keep to these rules, and one draw needn't show every extreme that they name: `prefix_len`: every group's live prefix is 1 to 2048 slots; in every draw some group's prefix fills all 2048 slots. `tail_len`: A request's live tail is 0 to 256 slots; in every draw some request's tail fills all 256 slots.
All inputs are finite; a program needn't handle non-finite values.
Results may differ from a plain program's by a relative error of at most 0.0075.
Values may be sent and summed in bfloat16 or wider, within the bound.
A program may use at most 128 MiB of HBM per device.

v0:
```python
import math
import jax
import jax.numpy as jnp
from jax import lax
from jax.sharding import PartitionSpec as P

D = 4096
H = 32
NEG = -1e30


def merged(value, axis, join):
    pieces = jax.tree.map(lambda part: lax.all_gather(part, axis), value)
    head = jax.tree.map(lambda part: part[0], pieces)
    tail = jax.tree.map(lambda part: part[1:], pieces)
    so_far, _ = lax.scan(lambda so_far, piece: (join(so_far, piece), None), head, tail)
    return so_far


def head_slopes(count):
    return jnp.power(2.0, -8.0 * (jnp.arange(count, dtype=jnp.float32) + 1.0) / count)


def attend(query_rows, key_block, value_block, query_pos, key_pos, key_mask):
    head_count = query_rows.shape[1]
    inv_scale = 1.0 / math.sqrt(query_rows.shape[2])
    scores = (
        jnp.einsum("qhd,khd->hqk", query_rows, key_block, preferred_element_type=jnp.float32)
        * inv_scale
    )
    distance = (query_pos[:, None] - key_pos[None, :]).astype(jnp.float32)
    scores = scores - head_slopes(head_count)[:, None, None] * distance[None, :, :]
    scores = jnp.where(key_mask, scores, NEG)
    row_max = jnp.max(scores, axis=2)
    weights = jnp.where(key_mask, jnp.exp(scores - row_max[:, :, None]), 0.0)
    weight_sum = jnp.sum(weights, axis=2)
    mixed_sum = jnp.einsum(
        "hqk,khd->qhd",
        weights.astype(jnp.bfloat16),
        value_block,
        preferred_element_type=jnp.float32,
    )
    return (row_max.T, weight_sum.T, mixed_sum)


def join_parts(first, second):
    best_max = jnp.maximum(first[0], second[0])
    factor_one = jnp.exp(first[0] - best_max)
    factor_two = jnp.exp(second[0] - best_max)
    return (
        best_max,
        first[1] * factor_one + second[1] * factor_two,
        first[2] * factor_one[:, :, None] + second[2] * factor_two[:, :, None],
    )


def body(
    queries,
    new_keys,
    new_values,
    prefix_keys,
    prefix_values,
    tail_keys,
    tail_values,
    prefix_len,
    tail_len,
    resid,
    w_out,
    ln_gain,
    w_up,
    w_down,
):
    group_req, step_count, model_width = queries.shape
    head_dim = model_width // H
    row_count = group_req * step_count
    seq_index = lax.axis_index("seq")
    core_index = lax.axis_index("mlp")
    block_len = prefix_keys.shape[1]
    tail_block = tail_keys.shape[1]
    block_start = (seq_index * lax.axis_size("mlp") + core_index) * block_len
    prefix_end = prefix_len[0]
    step_index = jnp.arange(step_count, dtype=jnp.int32)
    query_pos = prefix_end + jnp.repeat(tail_len, step_count) + jnp.tile(step_index, group_req)
    query_rows = queries.reshape(row_count, H, head_dim)
    key_pos = block_start + jnp.arange(block_len, dtype=jnp.int32)
    key_live = key_pos < prefix_end
    own_len = lax.dynamic_index_in_dim(tail_len, seq_index, 0, keepdims=False)
    own_rows = lax.dynamic_slice_in_dim(query_rows, seq_index * step_count, step_count, 0)
    own_pos = prefix_end + own_len + step_index
    tail_index = core_index * tail_block + jnp.arange(tail_block, dtype=jnp.int32)
    partial_value = attend(
        query_rows,
        prefix_keys[0].reshape(block_len, H, head_dim),
        prefix_values[0].reshape(block_len, H, head_dim),
        query_pos,
        key_pos,
        key_live[None, None, :],
    )
    tail_result = attend(
        own_rows,
        tail_keys[0].reshape(tail_block, H, head_dim),
        tail_values[0].reshape(tail_block, H, head_dim),
        own_pos,
        prefix_end + tail_index,
        (tail_index < own_len)[None, None, :],
    )
    self_mask = (step_index[None, :] <= step_index[:, None]) & (core_index == 0)
    self_result = attend(
        own_rows,
        new_keys[0].reshape(step_count, H, head_dim),
        new_values[0].reshape(step_count, H, head_dim),
        own_pos,
        own_pos,
        self_mask[None, :, :],
    )
    own_slice = tuple(
        (
            lax.dynamic_slice_in_dim(member, seq_index * step_count, step_count, 0)
            for member in partial_value
        )
    )
    own_part = join_parts(join_parts(own_slice, tail_result), self_result)
    partial_value = tuple(
        (
            lax.dynamic_update_slice_in_dim(member, update, seq_index * step_count, 0)
            for member, update in zip(partial_value, own_part)
        )
    )
    row_max, weight_sum, mixed_sum = merged(
        (partial_value[0], partial_value[1], partial_value[2]), ("seq", "mlp"), join_parts
    )
    attention = (
        (mixed_sum / weight_sum[:, :, None]).astype(jnp.bfloat16).reshape(row_count, model_width)
    )
    width_block = resid.shape[2]
    stream = resid.astype(jnp.float32).reshape(row_count, width_block) + jnp.dot(
        attention, w_out, preferred_element_type=jnp.float32
    )
    row_sums, squares = lax.psum(
        (jnp.sum(stream, axis=1), jnp.sum(stream * stream, axis=1)), ("seq", "mlp")
    )
    row_mean = row_sums / D
    row_var = squares / D - row_mean * row_mean
    hidden = (
        (stream - row_mean[:, None])
        * lax.rsqrt(row_var[:, None] + 1e-05)
        * ln_gain.astype(jnp.float32)
    ).astype(jnp.bfloat16)
    lifted = jnp.dot(
        lax.all_gather(hidden, "grp", axis=0, tiled=True), w_up, preferred_element_type=jnp.float32
    )
    summed = lax.psum(lifted, ("seq", "mlp"))
    activated = jax.nn.gelu(summed, approximate=False).astype(jnp.bfloat16)
    projected = lax.psum_scatter(
        jnp.dot(activated, w_down, preferred_element_type=jnp.float32),
        "grp",
        scatter_dimension=0,
        tiled=True,
    )
    return (stream + projected).reshape(group_req, step_count, width_block)


def solution(mesh):
    return jax.shard_map(
        body,
        mesh=mesh,
        in_specs=(
            P("grp", None, None),
            P(("grp", "seq"), None, None),
            P(("grp", "seq"), None, None),
            P("grp", ("seq", "mlp"), None),
            P("grp", ("seq", "mlp"), None),
            P(("grp", "seq"), "mlp", None),
            P(("grp", "seq"), "mlp", None),
            P("grp"),
            P("grp"),
            P("grp", None, ("seq", "mlp")),
            P(None, ("seq", "mlp")),
            P(("seq", "mlp")),
            P(("seq", "mlp"), "grp"),
            P("grp", ("seq", "mlp")),
        ),
        out_specs=P("grp", None, ("seq", "mlp")),
        check_vma=False,
    )
```

profile of v0, /device:TPU:0, one launch (start us, length us, event | category | flops | bytes accessed | tf_op | source)
XLA Modules:
  0.0 181.5 jit_solution(5606925134826433128)
XLA Ops:
  7.4 1.2 dynamic_slice.28
  9.2 0.6 fusion.102
  9.9 1.1 reshape.182
  11.0 1.4 copy.98
  12.5 0.7 fusion.143
  13.8 0.5 copy.97
  14.4 1.2 fusion.142
  16.9 0.5 copy.99
  17.4 1.0 fusion.3
  19.1 0.5 fusion.22
  19.8 0.8 copy.92
  21.0 15.8 %all_gather.32 = f32[8,16,32]{2,1,0:T(8,128)S(1)} all-gather(f32[1,16,32]{2,1,0:T(8,128)S(1)} %copy.83), channel_id=1, replica_groups=mesh['grp'=4,'seq'=4,'mlp'=2] {'seq','mlp'}, dimensions={0}, use_global_device_ids=true | all-gather | bytes 18432 | tf_op jit(solution)/shard_map/all_gather | solution.py:13
  37.2 14.1 %all_gather.29 = f32[8,16,32]{2,1,0:T(8,128)S(1)} all-gather(f32[1,16,32]{2,1,0:T(8,128)S(1)} %copy.76), channel_id=1, replica_groups=mesh['grp'=4,'seq'=4,'mlp'=2] {'seq','mlp'}, dimensions={0}, use_global_device_ids=true | all-gather | bytes 18432 | tf_op jit(solution)/shard_map/all_gather | solution.py:13
  51.4 1.7 all-gather.2.cloned.1.call-done
  53.1 1.7 slice.29
  54.8 1.0 slice_bitcast_fusion
  55.8 2.2 %while.14 = (s32[]{:T(128)}, f32[16,32]{1,0:T(8,128)S(1)}, f32[16,32]{1,0:T(8,128)S(1)}, f32[16,32,128]{2,1,0:T(8,128)S(1)}, f32[7,16,32]{2,1,0:T(8,128)S(1)}, /...) while((s32[]{:T(128)}, f32[16,32]{1,0:T(8,128)S(1)}, f32[16,32]{1,0:T(8,128)S(1)}, ...), condition=%wide.region_7.8_spmd, body=%wide.region_6.7_spmd.sunk | while | flops 199682 | bytes 807005 | solution.py:16
  55.8 0.3 fusion.153
  56.1 0.3 fusion.153
  56.4 0.3 fusion.153
  56.8 0.3 fusion.153
  57.1 0.3 fusion.153
  57.4 0.3 fusion.153
  58.1 3.0 %fusion.137 = (f32[16]{0:T(128)S(1)}, f32[16]{0:T(128)S(1)}, f32[16,512]{1,0:T(8,128)S(1)}) fusion(f32[16,512]{1,0:T(8,128)S(1)} %reshape.186, bf16[4096,512]{1,0:T(8,128)(2,1)} %param.26, bf16[2,8,32,128]{3,2,1,0:T(8,128)(2,1)S(1)} %bitcast.177), kind=kOutput, calls=%fused_computation.181 | convolution fusion | flops 67141600 | bytes 4391040 | tf_op jit(solution)/shard_map/dot_general | solution.py:136
  61.1 15.5 %all-reduce = (f32[16]{0:T(128)S(1)}, f32[16]{0:T(128)S(1)}) all-reduce(f32[16]{0:T(128)S(1)} %get-tuple-element.60, f32[16]{0:T(128)S(1)} %get-tuple-element.59), channel_id=1, replica_groups=mesh['grp'=4,'seq'=4,'mlp'=2] {'seq','mlp'}, use_global_device_ids=true, to_apply=%region_11.12 | all-reduce | flops 32 | bytes 256 | tf_op jit(solution)/shard_map/psum | solution.py:139
  76.6 8.1 %all_gather.36 = bf16[64,512]{1,0:T(8,128)(2,1)S(1)} all-gather(bf16[16,512]{1,0:T(8,128)(2,1)S(1)} %multiply_convert_fusion), channel_id=1, replica_groups=mesh['grp'=4,'seq'=4,'mlp'=2] {'grp'}, dimensions={0}, use_global_device_ids=true | all-gather | bytes 81920 | tf_op jit(solution)/shard_map/all_gather | solution.py:150
  84.8 4.1 %fusion.144 = f32[64,4096]{1,0:T(8,128)} fusion(bf16[64,512]{1,0:T(8,128)(2,1)S(1)} %all_gather.36, bf16[512,4096]{1,0:T(8,128)(2,1)} %param.28), kind=kOutput, calls=%fused_computation.184 | convolution fusion | flops 268435456 | bytes 5308416 | tf_op jit(solution)/shard_map/dot_general | solution.py:149
  88.9 56.1 %all-reduce.3.cloned.1.call-done = f32[64,4096]{1,0:T(8,128)} async-done(((f32[64,4096]{1,0:T(8,128)}), f32[64,4096]{1,0:T(8,128)}) %all-reduce.3.cloned.1.call-update) | async-done | bytes 1048592 | tf_op jit(solution)/shard_map/psum | solution.py:152
  145.1 5.5 %fusion.37 = f32[64,512]{1,0:T(8,128)} fusion(bf16[4096,512]{1,0:T(8,128)(2,1)} %param.29, f32[64,4096]{1,0:T(8,128)} %all-reduce.3.cloned.1.call-done), kind=kOutput, calls=%fused_computation.49 | convolution fusion | flops 285474816 | bytes 5373952 | tf_op jit(solution)/shard_map/dot_general | solution.py:155
  150.6 22.9 %reduce-scatter.2.cloned.1.call-done = f32[16,512]{1,0:T(8,128)} async-done(((f32[64,512]{1,0:T(8,128)}), f32[16,512]{1,0:T(8,128)}) %reduce-scatter.2.cloned.1.call-update) | async-done | bytes 32784 | tf_op jit(solution)/shard_map/reduce_scatter | solution.py:154
  173.6 0.8 add.168
  174.3 0.6 reshape.184
  (77 shorter events, 4.4 us)
Async XLA Ops:
  6.5 13.1 %copy-start = (bf16[1,4,4096]{2,1,0:T(4,128)(2,1)S(1)}, bf16[1,4,4096]{2,1,0:T(4,128)(2,1)}, u32[]{:S(2)}) copy-start(bf16[1,4,4096]{2,1,0:T(4,128)(2,1)} %param.18) | copy-start | bytes 98308
  6.5 7.1 %copy-start.7 = (s32[4]{0:T(128)S(1)}, s32[4]{0:T(128)}, u32[]{:S(2)}) copy-start(s32[4]{0:T(128)} %param.24) | copy-start | bytes 52
  6.5 7.2 %copy-start.1 = (bf16[1,256,4096]{2,1,0:T(8,128)(2,1)S(1)}, bf16[1,256,4096]{2,1,0:T(8,128)(2,1)}, u32[]{:S(2)}) copy-start(bf16[1,256,4096]{2,1,0:T(8,128)(2,1)} %param.19) | copy-start | bytes 6291460
  6.5 46.6 %all-gather.2.cloned.1.call-start = ((), (), s32[]{:S(2)}) async-start(), calls=%async_computation.1 | async-start | bytes 2359296 | tf_op jit(solution)/shard_map/all_gather | solution.py:13
  14.3 1.8 copy-start.4
  14.3 2.6 %copy-start.2 = (bf16[1,256,4096]{2,1,0:T(8,128)(2,1)S(1)}, bf16[1,256,4096]{2,1,0:T(8,128)(2,1)}, u32[]{:S(2)}) copy-start(bf16[1,256,4096]{2,1,0:T(8,128)(2,1)} %param.20) | copy-start | bytes 6291460
  17.3 1.2 copy-start.3
  18.8 32.5 %copy-start.5 = (bf16[4,4,512]{2,1,0:T(4,128)(2,1)S(1)}, bf16[4,4,512]{2,1,0:T(4,128)(2,1)}, u32[]{:S(2)}) copy-start(bf16[4,4,512]{2,1,0:T(4,128)(2,1)} %param.25) | copy-start | bytes 49156
  18.8 32.5 %copy-start.6 = (bf16[512]{0:T(512)(128)(2,1)S(1)}, bf16[512]{0:T(512)(128)(2,1)}, u32[]{:S(2)}) copy-start(bf16[512]{0:T(512)(128)(2,1)} %param.27) | copy-start | bytes 3076
  20.6 124.4 %all-reduce.3.cloned.1.call-start = ((), (), s32[]{:S(2)}) async-start(), calls=%async_computation.2 | async-start | bytes 2097152 | tf_op jit(solution)/shard_map/psum | solution.py:152
  88.9 84.7 %reduce-scatter.2.cloned.1.call-start = ((), (), s32[]{:S(2)}) async-start(), calls=%async_computation.3 | async-start | bytes 163840 | tf_op jit(solution)/shard_map/reduce_scatter | solution.py:154
Sparse Core Ops, SparseCore 0:
  20.8 32.3 all-gather.1
  89.0 56.0 all-reduce.2
  150.7 22.7 reduce-scatter.1
where the time goes:
time: 182 us; the launch traced here: 181 us
  waiting for transfers between devices  80.9 us (44%)
  blocking collectives  53.5 us (29%)
  matrix products  16.5 us (9%)
  between operations  14.8 us (8%)
  local copies, waits for them, and re-layouts  11 us (6%)
  other arithmetic  4.55 us (2%)
    psum x1, waiting for transfers between devices, body(): summed = lax.psum(lifted, ('seq', 'mlp'))  56.1 us
    all_gather x2, blocking collectives, merged(): pieces = jax.tree.map(lambda part: lax.all_gather(part, axis), value)  29.9 us
    reduce_scatter x1, waiting for transfers between devices, body(): lax.psum_scatter(jnp.dot(activated, w_down, preferred_element_type=jnp.fl...  22.9 us
    psum x1, blocking collectives, body(): lax.psum((jnp.sum(stream, axis=1), jnp.sum(stream * stream, axis=1)), ('s...  15.5 us
    all_gather x1, blocking collectives, body(): lax.all_gather(hidden, 'grp', axis=0, tiled=True)  8.13 us
    dot_general x1, matrix products, body(): jnp.dot(activated, w_down, preferred_element_type=jnp.float32)  5.52 us
    dot_general x1, matrix products, body(): jnp.dot(lax.all_gather(hidden, 'grp', axis=0, tiled=True), w_up, preferre...  4.1 us
  transfers between devices with their start and end apart: 3, of which 3 were waited for; matrix products, arithmetic and copies ran while one was open for 0% of the time, Pallas kernels for 0%

commit v1 on v0

--- a/solution.py
+++ b/solution.py
@@ -7,6 +7,14 @@
 D = 4096
 H = 32
 NEG = -1e30
+
+
+def refer_the_array(array_in, ndim_at):
+    array_in = jnp.moveaxis(array_in, 0, ndim_at)
+    row_out = array_in.shape
+    return array_in.reshape(
+        *row_out[:ndim_at], row_out[ndim_at] * row_out[ndim_at + 1], *row_out[ndim_at + 2 :]
+    )
 
 
 def merged(value, axis, join):
@@ -146,9 +154,28 @@
         * lax.rsqrt(row_var[:, None] + 1e-05)
         * ln_gain.astype(jnp.float32)
     ).astype(jnp.bfloat16)
-    lifted = jnp.dot(
-        lax.all_gather(hidden, "grp", axis=0, tiled=True), w_up, preferred_element_type=jnp.float32
-    )
+
+    def point_matrix(dim_at, field, ax_name):
+        k_all = lax.psum(1, ax_name)
+        store = [(ii, (ii + 1) % k_all) for ii in range(k_all)]
+        made = [(d, i) for i, d in store]
+        base_arr, part_now = ([], [])
+        for no in range(k_all - 1):
+            if no % 2 == 0:
+                v1 = lax.ppermute(base_arr[-1] if base_arr else field, ax_name, perm=store)
+                base_arr.append(v1)
+            else:
+                part_now.append(
+                    lax.ppermute(part_now[-1] if part_now else field, ax_name, perm=made)
+                )
+        main = jnp.stack([*base_arr[::-1], field, *part_now])
+        big = lax.axis_index(ax_name)
+        placed = len(base_arr)
+        front = big - placed
+        main = main[(jnp.arange(k_all) - front) % k_all]
+        return refer_the_array(main, dim_at)
+
+    lifted = jnp.dot(point_matrix(0, hidden, "grp"), w_up, preferred_element_type=jnp.float32)
     summed = lax.psum(lifted, ("seq", "mlp"))
     activated = jax.nn.gelu(summed, approximate=False).astype(jnp.bfloat16)
     projected = lax.psum_scatter(

time: 182 us -> 184 us (1.011)
  blocking collectives: 53.5 us -> 45.4 us
  waiting for transfers between devices: 80.9 us -> 86.6 us
  starting transfers between devices: 0.09 us -> 3.52 us
    all_gather x1 -> x0, blocking collectives: 8.13 us -> none  [body(): lax.all_gather(hidden, 'grp', axis=0, tiled=True)]
    ppermute x0 -> x3, waiting for transfers between devices: none -> 5.76 us  [the longest x2 5.74 us: point_matrix(): v1 = lax.ppermute(base_arr[-1] if base_arr else field, ax_name, perm=store)]
    ppermute x0 -> x3, starting transfers between devices: none -> 3.44 us  [the longest x2 1.92 us: point_matrix(): v1 = lax.ppermute(base_arr[-1] if base_arr else field, ax_name, perm=store)]
  transfers between devices with their start and end apart: 3 -> 6, of which waited for: 3 -> 5; matrix products, arithmetic and copies ran while one was open for 0% -> 0% of each run, Pallas kernels for 0% -> 0%
where the time goes in v1:
time: 184 us; the launch traced here: 183 us
  waiting for transfers between devices  86.6 us (47%)
  blocking collectives  45.4 us (25%)
  matrix products  16.4 us (9%)
  between operations  14.8 us (8%)
  local copies, waits for them, and re-layouts  11.6 us (6%)
  other arithmetic  4.66 us (3%)
  starting transfers between devices  3.52 us (2%)
    psum x1, waiting for transfers between devices, body(): summed = lax.psum(lifted, ('seq', 'mlp'))  56.1 us
    all_gather x2, blocking collectives, merged(): pieces = jax.tree.map(lambda part: lax.all_gather(part, axis), value)  29.9 us
    reduce_scatter x1, waiting for transfers between devices, body(): lax.psum_scatter(jnp.dot(activated, w_down, preferred_element_type=jnp.fl...  22.9 us
    psum x1, blocking collectives, body(): lax.psum((jnp.sum(stream, axis=1), jnp.sum(stream * stream, axis=1)), ('s...  15.5 us
    ppermute x2, waiting for transfers between devices, point_matrix(): v1 = lax.ppermute(base_arr[-1] if base_arr else field, ax_name, perm=store)  5.74 us
    dot_general x1, matrix products, body(): jnp.dot(activated, w_down, preferred_element_type=jnp.float32)  5.52 us
    dot_general x1, matrix products, body(): jnp.dot(point_matrix(0, hidden, 'grp'), w_up, preferred_element_type=jnp....  4.07 us
  transfers between devices with their start and end apart: 6, of which 5 were waited for; matrix products, arithmetic and copies ran while one was open for 0% of the time, Pallas kernels for 0%

profile of v1, /device:TPU:0, one launch (start us, length us, event | category | flops | bytes accessed | tf_op | source)
XLA Modules:
  0.0 183.1 jit_solution(14550273696721715514)
XLA Ops:
  7.4 1.2 dynamic_slice.28
  9.2 0.6 fusion.104
  9.9 1.1 reshape.234
  11.0 1.4 copy.98
  12.5 0.7 fusion.145
  13.8 0.5 copy.97
  14.4 1.2 fusion.144
  16.9 0.5 copy.99
  17.4 1.0 fusion.3
  19.1 0.5 fusion.22
  19.8 0.8 copy.92
  21.0 15.8 %all_gather.29 = f32[8,16,32]{2,1,0:T(8,128)S(1)} all-gather(f32[1,16,32]{2,1,0:T(8,128)S(1)} %copy.83), channel_id=1, replica_groups=mesh['grp'=4,'seq'=4,'mlp'=2] {'seq','mlp'}, dimensions={0}, use_global_device_ids=true | all-gather | bytes 18432 | tf_op jit(solution)/shard_map/all_gather | solution.py:21
  37.2 14.1 %all_gather.26 = f32[8,16,32]{2,1,0:T(8,128)S(1)} all-gather(f32[1,16,32]{2,1,0:T(8,128)S(1)} %copy.76), channel_id=1, replica_groups=mesh['grp'=4,'seq'=4,'mlp'=2] {'seq','mlp'}, dimensions={0}, use_global_device_ids=true | all-gather | bytes 18432 | tf_op jit(solution)/shard_map/all_gather | solution.py:21
  51.4 1.7 all-gather.2.cloned.1.call-done
  53.1 1.7 slice.31
  54.8 1.0 slice_bitcast_fusion
  55.8 2.2 %while.14 = (s32[]{:T(128)}, f32[16,32]{1,0:T(8,128)S(1)}, f32[16,32]{1,0:T(8,128)S(1)}, f32[16,32,128]{2,1,0:T(8,128)S(1)}, f32[7,16,32]{2,1,0:T(8,128)S(1)}, /...) while((s32[]{:T(128)}, f32[16,32]{1,0:T(8,128)S(1)}, f32[16,32]{1,0:T(8,128)S(1)}, ...), condition=%wide.region_7.8_spmd, body=%wide.region_6.7_spmd.sunk | while | flops 199682 | bytes 807005 | solution.py:24
  55.8 0.3 fusion.156
  58.1 3.0 %fusion.139 = (f32[16]{0:T(128)S(1)}, f32[16]{0:T(128)S(1)}, f32[16,512]{1,0:T(8,128)S(1)}) fusion(f32[16,512]{1,0:T(8,128)S(1)} %reshape.239, bf16[4096,512]{1,0:T(8,128)(2,1)} %param.26, bf16[2,8,32,128]{3,2,1,0:T(8,128)(2,1)S(1)} %bitcast.185), kind=kOutput, calls=%fused_computation.190 | convolution fusion | flops 67141600 | bytes 4391040 | tf_op jit(solution)/shard_map/dot_general | solution.py:144
  61.1 15.5 %all-reduce = (f32[16]{0:T(128)S(1)}, f32[16]{0:T(128)S(1)}) all-reduce(f32[16]{0:T(128)S(1)} %get-tuple-element.60, f32[16]{0:T(128)S(1)} %get-tuple-element.59), channel_id=1, replica_groups=mesh['grp'=4,'seq'=4,'mlp'=2] {'seq','mlp'}, use_global_device_ids=true, to_apply=%region_11.12 | all-reduce | flops 32 | bytes 256 | tf_op jit(solution)/shard_map/psum | solution.py:147
  76.6 1.4 collective-permute-start
  78.0 1.5 collective-permute-start.2
  79.6 1.7 collective-permute-done
  81.3 0.5 collective-permute-start.1
  81.9 4.0 %collective-permute-done.1 = bf16[16,512]{1,0:T(8,128)(2,1)S(1)} collective-permute-done((bf16[16,512]{1,0:T(8,128)(2,1)S(1)}, bf16[16,512]{1,0:T(8,128)(2,1)S(1)}, u32[]{:S(2)}, u32[]{:S(2)}) %collective-permute-start.1) | collective-permute-done | bytes 16416 | tf_op jit(solution)/shard_map/ppermute | solution.py:165
  85.9 0.6 gather_fusion
  86.5 4.1 %fusion.146 = f32[64,4096]{1,0:T(8,128)} fusion(bf16[64,512]{1,0:T(8,128)(2,1)S(1)} %bitcast.187, bf16[512,4096]{1,0:T(8,128)(2,1)} %param.28), kind=kOutput, calls=%fused_computation.193 | convolution fusion | flops 268435456 | bytes 5308416 | tf_op jit(solution)/shard_map/dot_general | solution.py:178
  90.6 56.1 %all-reduce.3.cloned.1.call-done = f32[64,4096]{1,0:T(8,128)} async-done(((f32[64,4096]{1,0:T(8,128)}), f32[64,4096]{1,0:T(8,128)}) %all-reduce.3.cloned.1.call-update) | async-done | bytes 1048592 | tf_op jit(solution)/shard_map/psum | solution.py:179
  146.7 5.5 %fusion.37 = f32[64,512]{1,0:T(8,128)} fusion(bf16[4096,512]{1,0:T(8,128)(2,1)} %param.29, f32[64,4096]{1,0:T(8,128)} %all-reduce.3.cloned.1.call-done), kind=kOutput, calls=%fused_computation.50 | convolution fusion | flops 285474816 | bytes 5373952 | tf_op jit(solution)/shard_map/dot_general | solution.py:182
  152.3 22.9 %reduce-scatter.2.cloned.1.call-done = f32[16,512]{1,0:T(8,128)} async-done(((f32[64,512]{1,0:T(8,128)}), f32[16,512]{1,0:T(8,128)}) %reduce-scatter.2.cloned.1.call-update) | async-done | bytes 32784 | tf_op jit(solution)/shard_map/reduce_scatter | solution.py:181
  175.2 0.8 add.194
  176.0 0.6 reshape.237
  (87 shorter events, 5.9 us)
Async XLA Ops:
  6.5 13.1 %copy-start = (bf16[1,4,4096]{2,1,0:T(4,128)(2,1)S(1)}, bf16[1,4,4096]{2,1,0:T(4,128)(2,1)}, u32[]{:S(2)}) copy-start(bf16[1,4,4096]{2,1,0:T(4,128)(2,1)} %param.18) | copy-start | bytes 98308
  6.5 7.1 %copy-start.7 = (s32[4]{0:T(128)S(1)}, s32[4]{0:T(128)}, u32[]{:S(2)}) copy-start(s32[4]{0:T(128)} %param.24) | copy-start | bytes 52
  6.5 7.2 %copy-start.1 = (bf16[1,256,4096]{2,1,0:T(8,128)(2,1)S(1)}, bf16[1,256,4096]{2,1,0:T(8,128)(2,1)}, u32[]{:S(2)}) copy-start(bf16[1,256,4096]{2,1,0:T(8,128)(2,1)} %param.19) | copy-start | bytes 6291460
  6.5 46.6 %all-gather.2.cloned.1.call-start = ((), (), s32[]{:S(2)}) async-start(), calls=%async_computation.1 | async-start | bytes 2359296 | tf_op jit(solution)/shard_map/all_gather | solution.py:21
  14.3 1.8 copy-start.4
  14.3 2.6 %copy-start.2 = (bf16[1,256,4096]{2,1,0:T(8,128)(2,1)S(1)}, bf16[1,256,4096]{2,1,0:T(8,128)(2,1)}, u32[]{:S(2)}) copy-start(bf16[1,256,4096]{2,1,0:T(8,128)(2,1)} %param.20) | copy-start | bytes 6291460
  17.4 1.2 copy-start.3
  18.8 32.5 %copy-start.5 = (bf16[4,4,512]{2,1,0:T(4,128)(2,1)S(1)}, bf16[4,4,512]{2,1,0:T(4,128)(2,1)}, u32[]{:S(2)}) copy-start(bf16[4,4,512]{2,1,0:T(4,128)(2,1)} %param.25) | copy-start | bytes 49156
  18.8 32.5 %copy-start.6 = (bf16[512]{0:T(512)(128)(2,1)S(1)}, bf16[512]{0:T(512)(128)(2,1)}, u32[]{:S(2)}) copy-start(bf16[512]{0:T(512)(128)(2,1)} %param.27) | copy-start | bytes 3076
  20.6 126.1 %all-reduce.3.cloned.1.call-start = ((), (), s32[]{:S(2)}) async-start(), calls=%async_computation.2 | async-start | bytes 2097152 | tf_op jit(solution)/shard_map/psum | solution.py:179
  76.6 4.6 %collective-permute-start = (bf16[16,512]{1,0:T(8,128)(2,1)S(1)}, bf16[16,512]{1,0:T(8,128)(2,1)S(1)}, u32[]{:S(2)}, u32[]{:S(2)}) collective-permute-start(bf16[16,512]{1,0:T(8,128)(2,1)S(1)} %multiply_convert_fusion), channel_id=1, source_target_pairs={{0,8},{8,16},{16,24},{24,0},{1,9},{9,17},{17,25},{25,1},{2,10},{10... | collective-permute-start | bytes 49160 | tf_op jit(solution)/shard_map/ppermute | solution.py:165
  78.0 3.8 %collective-permute-start.2 = (bf16[16,512]{1,0:T(8,128)(2,1)S(1)}, bf16[16,512]{1,0:T(8,128)(2,1)S(1)}, u32[]{:S(2)}, u32[]{:S(2)}) collective-permute-start(bf16[16,512]{1,0:T(8,128)(2,1)S(1)} %multiply_convert_fusion), channel_id=1, source_target_pairs={{8,0},{16,8},{24,16},{0,24},{9,1},{17,9},{25,17},{1,25},{10,2},{18... | collective-permute-start | bytes 49160 | tf_op jit(solution)/shard_map/ppermute | solution.py:169
  81.3 4.6 %collective-permute-start.1 = (bf16[16,512]{1,0:T(8,128)(2,1)S(1)}, bf16[16,512]{1,0:T(8,128)(2,1)S(1)}, u32[]{:S(2)}, u32[]{:S(2)}) collective-permute-start(bf16[16,512]{1,0:T(8,128)(2,1)S(1)} %collective-permute-done), channel_id=1, source_target_pairs={{0,8},{8,16},{16,24},{24,0},{1,9},{9,17},{17,25},{25,1},{2,10},{10... | collective-permute-start | bytes 49160 | tf_op jit(solution)/shard_map/ppermute | solution.py:165
  90.6 84.6 %reduce-scatter.2.cloned.1.call-start = ((), (), s32[]{:S(2)}) async-start(), calls=%async_computation.3 | async-start | bytes 163840 | tf_op jit(solution)/shard_map/reduce_scatter | solution.py:181
Sparse Core Ops, SparseCore 0:
  20.8 32.3 all-gather.1
  90.7 55.9 all-reduce.2
  152.4 22.7 reduce-scatter.1
